TPU v7x, 512 devices: a whole 4x4x16 slice. The times are simulated.
512 devices in a mesh: seq: 32 (over z, y_lo), mp: 16 (over x, y_hi, core).
Axes of the slice: x: 4, y: 4 (y_hi: 2, y_lo: 2; y = y_hi * 2 + y_lo), z: 16, core: 2. Of those that a mesh axis runs over, the one named last changes fastest.
Arguments:
- queries: bfloat16 [16384, 8192], P('seq', 'mp'), may hold values from -6 to 6
- keys_in: bfloat16 [16384, 8192], P('seq', 'mp'), may hold values from -6 to 6
- values_in: bfloat16 [16384, 8192], P('seq', 'mp'), may hold values from -6 to 6
- residual: bfloat16 [16384, 8192], P('seq', 'mp')
- short_taps: bfloat16 [3, 7, 8192], P(None, None, 'mp'), may hold values from -2 to 2
- mr_filter: bfloat16 [128, 512], P('seq', 'mp'), may hold values from -0.5 to 0.5
- norm_gain: bfloat16 [8192], P('mp'), may hold values from 0.5 to 1.5
- predecessor: int32 [32], replicated, may hold values from -1 to 31, as said below
- stretch_lengths: int32 [32], replicated, may hold values from 1 to 512, as said below
Outputs:
- mixed: bfloat16 [16384, 8192], P('seq', 'mp')
- normed: bfloat16 [16384, 8192], P('seq', 'mp')
Inputs may be any that keep to these rules, and one draw needn't show every extreme that they name: predecessor[j] is the stretch holding the preceding 512 tokens of stretch j's genome, or -1 for a genome's first stretch; each stretch precedes at most one stretch, and the chains have no cycles. `stretch_lengths`: every stretch that precedes another stretch is full (512 valid tokens); valid tokens come first.
All inputs are finite; a program needn't handle non-finite values.
Results may differ from a plain program's by a relative error of at most 0.0049.
Values may be sent and summed in bfloat16 or wider, within the bound.
A program may use at most 64 MiB of HBM per device.

v0:
```python
import jax
import jax.numpy as jnp
from jax import lax
from jax.sharding import PartitionSpec as P

EPSILON = 1e-06


def featurize(extended, taps):
    length = extended.shape[0] - 8
    total = jnp.zeros((length, extended.shape[1]), jnp.float32)
    for offset in range(taps.shape[0]):
        total = total + taps[offset].astype(jnp.float32) * extended[
            8 - offset : 8 - offset + length
        ].astype(jnp.float32)
    return total


def toeplitz_blocks(filter_rows):
    tap_count = filter_rows.shape[0]
    group_count = filter_rows.shape[1]
    flipped = filter_rows[::-1].T
    pattern = jnp.concatenate(
        [
            jnp.zeros((group_count, 1), filter_rows.dtype),
            flipped,
            jnp.zeros((group_count, tap_count), filter_rows.dtype),
        ],
        axis=1,
    )
    tiled = jnp.tile(pattern, (1, tap_count))[:, : 2 * tap_count * tap_count]
    return tiled.reshape(group_count, tap_count, 2 * tap_count)


def long_conv(extended, filter_rows, group_size):
    tap_count = filter_rows.shape[0]
    length = extended.shape[0] - tap_count
    blocks = length // tap_count
    channels = extended.shape[1]
    pieces = extended.reshape(blocks + 1, tap_count, channels)
    windows = jnp.concatenate([pieces[:-1], pieces[1:]], axis=1).reshape(
        blocks, 2 * tap_count, channels // group_size, group_size
    )
    matrices = toeplitz_blocks(filter_rows)
    result = jnp.einsum("gij,bjgc->bigc", matrices, windows, preferred_element_type=jnp.float32)
    return result.reshape(length, channels)


def body(
    queries,
    keys_in,
    values_in,
    residual,
    short_taps,
    mr_filter,
    norm_gain,
    predecessor,
    stretch_lengths,
):
    row_count, width = queries.shape
    device = lax.axis_index("seq")
    filter_rows = lax.all_gather(mr_filter, "seq", axis=0, tiled=True)
    tap_count = filter_rows.shape[0]
    group_size = width // filter_rows.shape[1]
    blank = jnp.zeros((8, width), queries.dtype)
    key_feat = featurize(jnp.concatenate([blank, keys_in]), short_taps[1])
    value_feat = featurize(jnp.concatenate([blank, values_in]), short_taps[2])
    mixed_in = (key_feat * value_feat).astype(jnp.bfloat16)
    state_tail = mixed_in[row_count - tap_count :][None]
    raw_tail = jnp.concatenate(
        [queries[row_count - 8 :], keys_in[row_count - 8 :], values_in[row_count - 8 :]], axis=1
    )[None]
    source = predecessor[device]
    carry = (jnp.zeros_like(state_tail), jnp.zeros_like(raw_tail))
    piece = (
        lax.all_gather(state_tail, "seq", axis=0, tiled=True),
        lax.all_gather(raw_tail, "seq", axis=0, tiled=True),
    )
    count = piece[0].shape[0]
    inside = (source >= 0) & (source < count)
    offset = jnp.clip(source, 0, count - 1)
    prev_state, prev_raw = tuple(
        (
            jnp.where(inside, lax.dynamic_slice_in_dim(member, offset, 1, 0), kept)
            for member, kept in zip(piece, carry)
        )
    )
    prev_rows = prev_raw[0]
    prev_query = prev_rows[:, :width]
    prev_key = prev_rows[:, width : 2 * width]
    prev_value = prev_rows[:, 2 * width :]
    query_feat = featurize(jnp.concatenate([prev_query, queries]), short_taps[0])
    head_key = featurize(jnp.concatenate([prev_key, keys_in[:8]]), short_taps[1])
    head_value = featurize(jnp.concatenate([prev_value, values_in[:8]]), short_taps[2])
    head_mixed = (head_key * head_value).astype(jnp.bfloat16)
    mixed_in = jnp.concatenate([head_mixed, mixed_in[8:]])
    extended = jnp.concatenate([prev_state[0], mixed_in])
    filtered = long_conv(extended, filter_rows, group_size)
    valid = (jnp.arange(row_count, dtype=jnp.int32) < stretch_lengths[device])[:, None]
    mixed = jnp.where(valid, query_feat * filtered, 0.0).astype(jnp.bfloat16)
    summed = residual.astype(jnp.float32) + mixed.astype(jnp.float32)
    squares_total = lax.psum(jnp.sum(summed * summed, axis=1), "mp")
    scale_rows = lax.rsqrt(squares_total / (width * lax.axis_size("mp")) + EPSILON)
    normed = jnp.where(
        valid, summed * scale_rows[:, None] * norm_gain.astype(jnp.float32), 0.0
    ).astype(jnp.bfloat16)
    return (mixed, normed)


def solution(mesh):
    in_specs = (
        P("seq", "mp"),
        P("seq", "mp"),
        P("seq", "mp"),
        P("seq", "mp"),
        P(None, None, "mp"),
        P("seq", "mp"),
        P("mp"),
        P(),
        P(),
    )
    out_specs = (P("seq", "mp"), P("seq", "mp"))
    return jax.shard_map(body, mesh=mesh, in_specs=in_specs, out_specs=out_specs, check_vma=False)
```

profile of v0, /device:TPU:1, one launch (start us, length us, event | category | flops | bytes accessed | tf_op | source)
XLA Modules:
  0.0 226.0 jit_solution(18346637916515088260)
XLA Ops:
  7.2 1.0 slice_convert_fusion.20
  8.2 0.8 slice_convert_fusion.1
  9.0 5.3 %multiply_convert_fusion = bf16[512,512]{1,0:T(8,128)(2,1)S(1)} fusion(bf16[512,512]{1,0:T(8,128)(2,1)} %param.11, bf16[512,512]{1,0:T(8,128)(2,1)} %param.10, f32[512]{0:T(512)S(1)} %bitcast.92, f32[512]{0:T(512)S(1)} %bitcast.90, f32[512]{0:T(512)S(1)} %bitcast.66, f32[512]{0:T(512)S(1)} %bitcast.68, f32[512]{0:T(512)S(1)} %bitcast.70, ...), kind=kLoop, calls=%fused_computation.17 | loop fusion | flops 11010048 | bytes 1601536 | tf_op jit(solution)/shard_map/convert_element_type | solution.py:68
  14.4 0.7 slice.328
  16.9 1.0 copy.66
  18.5 56.7 %all-gather.2 = bf16[32,4,32]{2,1,0:T(4,128)(2,1)S(1)} all-gather(bf16[1,4,32]{2,1,0:T(4,128)(2,1)S(1)} %bitcast.102), channel_id=1, replica_groups=mesh['seq'=32,'mp'=16] {'seq'}, dimensions={0}, use_global_device_ids=true | all-gather | bytes 8448 | tf_op jit(solution)/shard_map/all_gather | solution.py:62
  75.8 4.4 %tile.10 = bf16[32,32896]{1,0:T(8,128)(2,1)} reshape(bf16[32,128,257]{2,1,0:T(8,128)(2,1)S(1)} %tile.4) | data formatting | bytes 4210688 | tf_op jit(solution)/shard_map/tile | solution.py:31
  80.3 1.6 slice-done
  82.4 0.8 fusion.27
  83.2 59.5 %all-gather = bf16[256,1536]{1,0:T(8,128)(2,1)S(1)} all-gather(bf16[8,1536]{1,0:T(8,128)(2,1)S(1)} %pad_maximum_fusion.4), channel_id=2, replica_groups=mesh['seq'=32,'mp'=16] {'seq'}, dimensions={0}, use_global_device_ids=true | all-gather | bytes 811008 | tf_op jit(solution)/shard_map/all_gather | solution.py:77
  143.6 1.3 copy.75
  145.7 4.9 %all-gather.5.cloned.1.call-done = bf16[4096,512]{1,0:T(8,128)(2,1)} async-done(((bf16[128,512]{1,0:T(8,128)(2,1)}), bf16[4096,512]{1,0:T(8,128)(2,1)}) %all-gather.5.cloned.1.call-update) | async-done | bytes 4194320 | tf_op jit(solution)/shard_map/all_gather | solution.py:76
  150.6 0.9 select_bitcast_fusion
  151.5 1.0 pad_maximum_fusion
  152.6 2.1 copy.69
  154.7 2.0 concatenate.42
  156.7 1.9 copy.71
  158.6 1.0 copy.70
  159.6 1.2 concatenate.44
  160.9 1.9 fusion.2
  163.8 2.1 multiply_reduce_fusion
  165.9 51.0 %psum.7 = f32[512]{0:T(512)S(1)} all-reduce(f32[512]{0:T(512)S(1)} %get-tuple-element.8), channel_id=1, replica_groups=mesh['seq'=32,'mp'=16] {'mp'}, use_global_device_ids=true, to_apply=%region_1.2 | all-reduce | flops 512 | bytes 4096 | tf_op jit(solution)/shard_map/psum | solution.py:102
  216.9 1.0 copy.76
  218.1 1.0 copy.77
  (44 shorter events, 4.8 us)
Async XLA Ops:
  7.2 8.0 %copy-start.6 = (s32[32]{0:T(128)S(1)}, s32[32]{0:T(128)}, u32[]{:S(2)}) copy-start(s32[32]{0:T(128)} %param.16) | copy-start | bytes 388
  7.2 9.7 %copy-start.3 = (bf16[512,512]{1,0:T(8,128)(2,1)S(1)}, bf16[512,512]{1,0:T(8,128)(2,1)}, u32[]{:S(2)}) copy-start(bf16[512,512]{1,0:T(8,128)(2,1)} %param.9) | copy-start | bytes 1572868
  7.2 143.4 %all-gather.5.cloned.1.call-start = ((), (), s32[]{:S(2)}) async-start(), calls=%async_computation | async-start | bytes 4325376 | tf_op jit(solution)/shard_map/all_gather | solution.py:76
  8.2 10.2 %copy-start.4 = (bf16[4,32]{1,0:T(4,128)(2,1)S(1)}, bf16[4,32]{1,0:T(4,128)(2,1)}, u32[]{:S(2)}) copy-start(bf16[4,32]{1,0:T(4,128)(2,1)} %param.14) | copy-start | bytes 772
  14.4 61.1 %copy-start = (bf16[512,512]{1,0:T(8,128)(2,1)}, bf16[512,512]{1,0:T(8,128)(2,1)S(1)}, u32[]{:S(2)}) copy-start(bf16[512,512]{1,0:T(8,128)(2,1)S(1)} %multiply_convert_fusion) | copy-start | bytes 1572868
  80.3 1.6 slice-start
  81.9 1.3 slice-start.2
  81.9 61.1 %copy-start.7 = (s32[32]{0:T(128)S(1)}, s32[32]{0:T(128)}, u32[]{:S(2)}) copy-start(s32[32]{0:T(128)} %param.17) | copy-start | bytes 388
  82.4 62.5 %copy-start.5 = (bf16[512]{0:T(512)(128)(2,1)S(1)}, bf16[512]{0:T(512)(128)(2,1)}, u32[]{:S(2)}) copy-start(bf16[512]{0:T(512)(128)(2,1)} %param.15) | copy-start | bytes 3076
  82.4 69.1 %slice-start.1 = ((bf16[512,512]{1,0:T(8,128)(2,1)}), bf16[504,512]{1,0:T(8,128)(2,1)S(1)}, s32[]{:S(2)}) async-start(bf16[512,512]{1,0:T(8,128)(2,1)} %copy-done), calls=%async_computation.2 | async-start | bytes 1032192 | tf_op jit(solution)/shard_map/slice | solution.py:96
  152.6 6.0 %copy-start.1 = (bf16[512,512]{1,0:T(8,128)(2,1)S(1)}, bf16[512,512]{1,0:T(8,128)(2,1)}, u32[]{:S(2)}) copy-start(bf16[512,512]{1,0:T(8,128)(2,1)} %get-tuple-element.11) | copy-start | bytes 1572868
  162.8 1.0 copy-start.2
Sparse Core Ops, SparseCore 0:
  15.3 135.2 all-gather.4
where the time goes:
time: 227 us; the launch traced here: 226 us
  blocking collectives  167 us (74%)
  local copies, waits for them, and re-layouts  23.7 us (10%)
  between operations  16 us (7%)
  other arithmetic  12.3 us (5%)
  waiting for transfers between devices  4.95 us (2%)
    all_gather x1, blocking collectives, body(): lax.all_gather(raw_tail, 'seq', axis=0, tiled=True)  59.5 us
    all_gather x1, blocking collectives, body(): filter_rows = lax.all_gather(mr_filter, 'seq', axis=0, tiled=True)  56.7 us
    psum x1, blocking collectives, body(): squares_total = lax.psum(jnp.sum(summed * summed, axis=1), 'mp')  51 us
    unnamed x22, local copies, waits for them, and re-layouts  5.46 us
    convert_element_type x1, other arithmetic, body(): mixed_in = (key_feat * value_feat).astype(jnp.bfloat16)  5.34 us
    concatenate x4, local copies, waits for them, and re-layouts, long_conv(): jnp.concatenate([pieces[:-1], pieces[1:]], axis=1)  5.16 us
    all_gather x1, waiting for transfers between devices, body(): lax.all_gather(state_tail, 'seq', axis=0, tiled=True)  4.93 us
    another operation x2, local copies, waits for them, and re-layouts, toeplitz_blocks(): tiled = jnp.tile(pattern, (1, tap_count))[:, :2 * tap_count * tap_count]  4.73 us
  transfers between devices with their start and end apart: 1, of which 1 were waited for; matrix products, arithmetic and copies ran while one was open for 5% of the time, Pallas kernels for 0%

commit v1 on v0

v1 whole, which is shorter than its diff:
```python
import functools

import jax
import jax.numpy as jnp
from jax import lax
from jax.experimental import pallas as pl
from jax.experimental.pallas import tpu as pltpu
from jax.sharding import PartitionSpec as P

MESH = pl.DeviceIdType.MESH
EPSILON = 1e-06
ROWS = 512
WIDTH = 512
LANES = 128
TAPS = 128
SHORT = 7
GSIZE = 16
PAD = 16
CHUNK = 64
SLOT = 20
F32 = jnp.float32
BF16 = jnp.bfloat16


def kernel(
    n_seq,
    n_mp,
    q_hbm,
    k_hbm,
    v_hbm,
    r_hbm,
    taps_hbm,
    filt_hbm,
    gain_hbm,
    pred_ref,
    len_ref,
    mixed_hbm,
    normed_hbm,
    qbuf,
    kbuf,
    vbuf,
    rbuf,
    tapsb,
    filtb,
    gainb,
    taps,
    qfeat,
    mix,
    msg,
    recv,
    fwd,
    fin,
    rows_f,
    toep,
    flipped,
    summed,
    squares,
    mixed_v,
    normed_v,
    part,
    parts,
    load_sem,
    store_sem,
    send1,
    recv1,
    send2,
    recv2,
    send3,
    recv3,
):
    me = lax.axis_index("seq")
    mine = lax.axis_index("mp")

    barrier = pltpu.get_barrier_semaphore()

    def hello_seq(d, _):
        pl.semaphore_signal(
            barrier, inc=1, device_id={"seq": lax.rem(me + d, n_seq)}, device_id_type=MESH
        )
        return 0

    def hello_mp(d, _):
        pl.semaphore_signal(
            barrier, inc=1, device_id={"mp": lax.rem(mine + d, n_mp)}, device_id_type=MESH
        )
        return 0

    lax.fori_loop(1, n_seq, hello_seq, 0)
    lax.fori_loop(1, n_mp, hello_mp, 0)

    body = pl.ds(PAD, ROWS)
    loads = [
        pltpu.make_async_copy(k_hbm, kbuf.at[body], load_sem.at[0]),
        pltpu.make_async_copy(v_hbm, vbuf.at[body], load_sem.at[1]),
        pltpu.make_async_copy(taps_hbm, tapsb, load_sem.at[2]),
        pltpu.make_async_copy(filt_hbm, filtb, load_sem.at[3]),
        pltpu.make_async_copy(q_hbm, qbuf.at[body], load_sem.at[4]),
        pltpu.make_async_copy(r_hbm, rbuf, load_sem.at[5]),
        pltpu.make_async_copy(gain_hbm, gainb, load_sem.at[6]),
    ]
    for load in loads:
        load.start()
    for ref in (qbuf, kbuf, vbuf):
        ref[0:PAD, :] = jnp.zeros((PAD, WIDTH), BF16)
    for load in loads[:4]:
        load.wait()
    for branch in range(3):
        taps[8 * branch : 8 * branch + SHORT, :] = tapsb[branch].astype(F32)

    def featurize(ref, branch, start, count, lanes):
        ext = ref[pl.ds(start, count + PAD), lanes].astype(F32)[PAD - 8 :]
        acc = taps[pl.ds(8 * branch, 1), lanes] * ext[8:]
        for s in range(1, SHORT):
            acc = acc + taps[pl.ds(8 * branch + s, 1), lanes] * pltpu.roll(ext, s, 0)[8:]
        return acc

    def product(start, count, lanes):
        key_feat = featurize(kbuf, 1, start, count, lanes)
        value_feat = featurize(vbuf, 2, start, count, lanes)
        return (key_feat * value_feat).astype(BF16)

    tiles = WIDTH // LANES
    per_tile = ROWS // CHUNK
    tail_chunks = TAPS // CHUNK

    def tail_step(c, _):
        for b in range(tiles):
            lanes = pl.ds(b * LANES, LANES)
            start = pl.multiple_of(ROWS - TAPS + c * CHUNK, CHUNK)
            value = product(start, CHUNK, lanes)
            mix[pl.ds(TAPS + start, CHUNK), lanes] = value
            for a in range(CHUNK // 16):
                msg[(c * (CHUNK // 16) + a) * tiles + b, 0:16, :] = value[16 * a : 16 * a + 16]
        return 0

    lax.fori_loop(0, tail_chunks, tail_step, 0)

    loads[4].wait()
    for i, ref in enumerate((qbuf, kbuf, vbuf)):
        tail = ref[PAD + ROWS - 16 : PAD + ROWS, :].astype(F32)[8:]
        for b in range(tiles):
            rows_f[pl.ds(4 * b + i, 8, stride=16), :] = tail[:, b * LANES : (b + 1) * LANES]
    filt = filtb[...].astype(F32)
    share, groups = filt.shape
    row = jnp.concatenate([filt[i : i + 1] for i in range(share)], axis=1)
    for b in range(tiles):
        rows_f[pl.ds(4 * b + 3, 8, stride=16), :] = jnp.broadcast_to(row, (8, LANES))

    def pack(p, _):
        msg[p, 16:20, :] = rows_f[pl.ds(pl.multiple_of(4 * p, 4), 4), :].astype(BF16)
        return 0

    lax.fori_loop(0, n_seq, pack, 0)
    recv[me] = msg[me]

    pl.semaphore_wait(barrier, n_seq + n_mp - 2)

    def scatter(d, _):
        p = lax.rem(me + d, n_seq)
        pltpu.make_async_remote_copy(
            src_ref=msg.at[p],
            dst_ref=recv.at[me],
            send_sem=send1,
            recv_sem=recv1,
            device_id={"seq": p},
            device_id_type=MESH,
        ).start()
        return 0

    lax.fori_loop(1, n_seq, scatter, 0)

    def rest_step(c, _):
        start = pl.multiple_of(c * CHUNK, CHUNK)
        for b in range(tiles):
            lanes = pl.ds(b * LANES, LANES)
            mix[pl.ds(TAPS + start, CHUNK), lanes] = product(start, CHUNK, lanes)
        return 0

    lax.fori_loop(0, per_tile - tail_chunks, rest_step, 0)

    def query_step(c, _):
        start = pl.multiple_of(c * CHUNK, CHUNK)
        for b in range(tiles):
            lanes = pl.ds(b * LANES, LANES)
            qfeat[pl.ds(start, CHUNK), lanes] = featurize(qbuf, 0, start, CHUNK, lanes)
        return 0

    lax.fori_loop(0, per_tile, query_step, 0)
    squares[...] = jnp.zeros((ROWS, LANES), F32)

    others = pl.ds(0, n_seq - 1)
    pltpu.make_async_copy(recv.at[others], recv.at[others], recv1).wait()

    def forward(i):
        source = pred_ref[i]
        keep = (source >= 0).astype(F32)
        piece = recv[jnp.maximum(source, 0)]
        return (piece.astype(F32) * keep).astype(BF16)

    def route(d, _):
        i = lax.rem(me + d, n_seq)
        fwd[i] = forward(i)
        pltpu.make_async_remote_copy(
            src_ref=fwd.at[i],
            dst_ref=fin.at[me],
            send_sem=send2,
            recv_sem=recv2,
            device_id={"seq": i},
            device_id_type=MESH,
        ).start()
        return 0

    lax.fori_loop(1, n_seq, route, 0)
    fin[me] = forward(me)

    def unpack_recv(p, _):
        rows_f[pl.ds(pl.multiple_of(4 * p, 4), 4), :] = recv[p, 16:20, :].astype(F32)
        return 0

    lax.fori_loop(0, n_seq, unpack_recv, 0)
    gathered = rows_f[pl.ds(3, n_seq, stride=4), :]
    stacked = jnp.concatenate(
        [gathered[:, i * groups : (i + 1) * groups] for i in range(share)], axis=0
    )
    at = lax.broadcasted_iota(jnp.int32, (TAPS, LANES), 0)
    tap = share * (at & (n_seq - 1)) + at // n_seq
    place = (TAPS - tap) & (TAPS - 1)
    spread = (place == lax.broadcasted_iota(jnp.int32, (TAPS, LANES), 1)).astype(BF16)
    flipped[...] = lax.dot_general(
        stacked.astype(BF16), spread, (((0,), (0,)), ((), ())), preferred_element_type=F32
    )
    below = lax.broadcasted_iota(jnp.int32, (TAPS, LANES), 1) <= lax.broadcasted_iota(
        jnp.int32, (TAPS, LANES), 0
    )

    def toeplitz(g, _):
        first = jnp.broadcast_to(flipped[pl.ds(g, 1), :], (TAPS, LANES))
        turned = pltpu.roll(first, 0, 1, stride=1, stride_axis=0)
        rows = pl.ds(pl.multiple_of(g * TAPS, TAPS), TAPS)
        toep[rows, 0:LANES] = jnp.where(below, 0.0, turned).astype(BF16)
        toep[rows, LANES : 2 * LANES] = jnp.where(below, turned, 0.0).astype(BF16)
        return 0

    lax.fori_loop(0, groups, toeplitz, 0)

    length = len_ref[me]
    loads[5].wait()
    loads[6].wait()
    in_tile = LANES // GSIZE
    lane_group = lax.broadcasted_iota(jnp.int32, (TAPS, LANES), 1) // GSIZE

    def convolve(pair):
        def step(b, _):
            lanes = pl.ds(pl.multiple_of(b * LANES, LANES), LANES)
            window = jnp.concatenate(
                [mix[blk * TAPS : (blk + 2) * TAPS, lanes] for blk in pair], axis=1
            )
            rows = pl.ds(pl.multiple_of(b * in_tile * TAPS, TAPS), in_tile * TAPS)
            product_all = jnp.dot(toep[rows, :], window, preferred_element_type=F32)
            for half, blk in enumerate(pair):
                side = slice(half * LANES, (half + 1) * LANES)
                out = product_all[0:TAPS, side]
                for g in range(1, in_tile):
                    out = jnp.where(
                        lane_group == g, product_all[g * TAPS : (g + 1) * TAPS, side], out
                    )
                span = slice(blk * TAPS, (blk + 1) * TAPS)
                valid = (
                    lax.broadcasted_iota(jnp.int32, (TAPS, LANES), 0) + blk * TAPS
                ) < length
                mixed = jnp.where(valid, qfeat[span, lanes] * out, 0.0).astype(BF16)
                mixed_v[span, lanes] = mixed
                total = rbuf[span, lanes].astype(F32) + mixed.astype(F32)
                summed[span, lanes] = total
                squares[span, :] = squares[span, :] + total * total
            return 0

        lax.fori_loop(0, tiles, step, 0)

    def store_pair(pair, sem):
        span = pl.ds(pair[0] * TAPS, len(pair) * TAPS)
        return pltpu.make_async_copy(mixed_v.at[span], mixed_hbm.at[span], sem)

    convolve((2, 3))
    stores = [store_pair((2, 3), store_sem.at[0])]
    stores[0].start()

    pltpu.make_async_copy(fin.at[others], fin.at[others], recv2).wait()

    def unpack_fin(p, _):
        rows_f[pl.ds(pl.multiple_of(4 * p, 4), 4), :] = fin[p, 16:20, :].astype(F32)
        return 0

    lax.fori_loop(0, n_seq, unpack_fin, 0)
    for a in range(TAPS // 16):
        for b in range(tiles):
            mix[16 * a : 16 * a + 16, b * LANES : (b + 1) * LANES] = fin[a * tiles + b, 0:16, :]
    for i, ref in enumerate((qbuf, kbuf, vbuf)):
        for b in range(tiles):
            head = rows_f[pl.ds(4 * b + i, 8, stride=16), :]
            ref[0:PAD, b * LANES : (b + 1) * LANES] = jnp.concatenate(
                [jnp.zeros_like(head), head], axis=0
            ).astype(BF16)
    for b in range(tiles):
        lanes = pl.ds(b * LANES, LANES)
        mix[TAPS : TAPS + 16, lanes] = product(0, 16, lanes)
        qfeat[0:16, lanes] = featurize(qbuf, 0, 0, 16, lanes)

    convolve((0, 1))
    stores.append(store_pair((0, 1), store_sem.at[1]))
    stores[1].start()

    for blk in range(ROWS // TAPS):
        span = slice(blk * TAPS, (blk + 1) * TAPS)
        part[:, span] = jnp.sum(squares[span, :].T, axis=0, keepdims=True)
    parts[mine] = part[...]

    def share_part(d, _):
        pltpu.make_async_remote_copy(
            src_ref=part,
            dst_ref=parts.at[mine],
            send_sem=send3,
            recv_sem=recv3,
            device_id={"mp": lax.rem(mine + d, n_mp)},
            device_id_type=MESH,
        ).start()
        return 0

    lax.fori_loop(1, n_mp, share_part, 0)
    if n_mp > 1:
        peers = pl.ds(0, n_mp - 1)
        pltpu.make_async_copy(parts.at[peers], parts.at[peers], recv3).wait()
    total = jnp.sum(parts[...], axis=0)
    scale = lax.rsqrt(total / (WIDTH * n_mp) + EPSILON)
    gain = gainb[...].astype(F32)
    for blk in range(ROWS // TAPS):
        span = slice(blk * TAPS, (blk + 1) * TAPS)
        column = jnp.broadcast_to(scale[:, span], (TAPS, LANES)).T
        valid = (lax.broadcasted_iota(jnp.int32, (TAPS, LANES), 0) + blk * TAPS) < length
        for b in range(tiles):
            lanes = slice(b * LANES, (b + 1) * LANES)
            normed_v[span, lanes] = jnp.where(
                valid, summed[span, lanes] * column * gain[:, lanes], 0.0
            ).astype(BF16)
        part_rows = pl.ds(blk * TAPS, TAPS)
        stores.append(
            pltpu.make_async_copy(
                normed_v.at[part_rows], normed_hbm.at[part_rows], store_sem.at[2 + blk]
            )
        )
        stores[-1].start()

    pltpu.make_async_copy(msg.at[others], msg.at[others], send1).wait()
    pltpu.make_async_copy(fwd.at[others], fwd.at[others], send2).wait()
    if n_mp > 1:
        pltpu.make_async_copy(parts.at[peers], parts.at[peers], send3).wait()
    for store in stores:
        store.wait()


def body(n_seq, n_mp, queries, keys_in, values_in, residual, short_taps, mr_filter, norm_gain, predecessor, stretch_lengths):
    whole = pl.BlockSpec(memory_space=pl.ANY)
    scalars = pl.BlockSpec(memory_space=pltpu.SMEM)
    slots = (n_seq, SLOT, LANES)
    share, groups = mr_filter.shape
    out = jax.ShapeDtypeStruct((ROWS, WIDTH), BF16)
    return pl.pallas_call(
        functools.partial(kernel, n_seq, n_mp),
        out_shape=(out, out),
        in_specs=[whole] * 7 + [scalars] * 2,
        out_specs=(whole, whole),
        scratch_shapes=[
            pltpu.VMEM((PAD + ROWS, WIDTH), BF16),
            pltpu.VMEM((PAD + ROWS, WIDTH), BF16),
            pltpu.VMEM((PAD + ROWS, WIDTH), BF16),
            pltpu.VMEM((ROWS, WIDTH), BF16),
            pltpu.VMEM((3, SHORT, WIDTH), BF16),
            pltpu.VMEM((share, groups), BF16),
            pltpu.VMEM((1, WIDTH), BF16),
            pltpu.VMEM((24, WIDTH), F32),
            pltpu.VMEM((ROWS, WIDTH), F32),
            pltpu.VMEM((TAPS + ROWS, WIDTH), BF16),
            pltpu.VMEM(slots, BF16),
            pltpu.VMEM(slots, BF16),
            pltpu.VMEM(slots, BF16),
            pltpu.VMEM(slots, BF16),
            pltpu.VMEM((LANES, LANES), F32),
            pltpu.VMEM((groups * TAPS, 2 * TAPS), BF16),
            pltpu.VMEM((groups, LANES), F32),
            pltpu.VMEM((ROWS, WIDTH), F32),
            pltpu.VMEM((ROWS, LANES), F32),
            pltpu.VMEM((ROWS, WIDTH), BF16),
            pltpu.VMEM((ROWS, WIDTH), BF16),
            pltpu.VMEM((1, ROWS), F32),
            pltpu.VMEM((n_mp, 1, ROWS), F32),
            pltpu.SemaphoreType.DMA((7,)),
            pltpu.SemaphoreType.DMA((6,)),
            pltpu.SemaphoreType.DMA,
            pltpu.SemaphoreType.DMA,
            pltpu.SemaphoreType.DMA,
            pltpu.SemaphoreType.DMA,
            pltpu.SemaphoreType.DMA,
            pltpu.SemaphoreType.DMA,
        ],
        compiler_params=pltpu.CompilerParams(
            collective_id=0, has_side_effects=True, vmem_limit_bytes=40 * 1024 * 1024
        ),
    )(
        queries,
        keys_in,
        values_in,
        residual,
        short_taps,
        mr_filter,
        norm_gain.reshape(1, WIDTH),
        predecessor,
        stretch_lengths,
    )


def solution(mesh):
    in_specs = (
        P("seq", "mp"),
        P("seq", "mp"),
        P("seq", "mp"),
        P("seq", "mp"),
        P(None, None, "mp"),
        P("seq", "mp"),
        P("mp"),
        P(),
        P(),
    )
    out_specs = (P("seq", "mp"), P("seq", "mp"))
    return jax.shard_map(
        functools.partial(body, mesh.shape["seq"], mesh.shape["mp"]),
        mesh=mesh,
        in_specs=in_specs,
        out_specs=out_specs,
        check_vma=False,
    )
```

time: 227 us -> 60.8 us (0.27)
  blocking collectives: 167 us -> 0 us
  Pallas kernels: 0 us -> 52.6 us
  local copies, waits for them, and re-layouts: 23.7 us -> 7.2 us
  between operations: 16 us -> 0.68 us
  other arithmetic: 12.3 us -> 0 us
  waiting for transfers between devices: 4.95 us -> 0 us
    all_gather x2 -> x0, blocking collectives: 116 us -> none  [the longest x1 59.5 us: body(): lax.all_gather(raw_tail, 'seq', axis=0, tiled=True)]
    pallas_call x0 -> x1, Pallas kernels: none -> 52.6 us  [body(): pl.pallas_call(functools.partial(kernel, n_seq, n_mp), out_shape=(out, ou...]
    psum x1 -> x0, blocking collectives: 51 us -> none  [body(): squares_total = lax.psum(jnp.sum(summed * summed, axis=1), 'mp')]
    convert_element_type x6 -> x0, other arithmetic: 7.43 us -> none  [the longest x1 5.34 us: body(): mixed_in = (key_feat * value_feat).astype(jnp.bfloat16)]
    concatenate x7 -> x0, local copies, waits for them, and re-layouts: 6.26 us -> none  [the longest x4 5.16 us: long_conv(): jnp.concatenate([pieces[:-1], pieces[1:]], axis=1)]
    slice x11 -> x0, local copies, waits for them, and re-layouts: 5.44 us -> none  [the longest x1 2.12 us: long_conv(): pieces[:-1]]
    all_gather x1 -> x0, waiting for transfers between devices: 4.93 us -> none  [body(): lax.all_gather(state_tail, 'seq', axis=0, tiled=True)]
    another operation x2 -> x0, local copies, waits for them, and re-layouts: 4.73 us -> none  [toeplitz_blocks(): tiled = jnp.tile(pattern, (1, tap_count))[:, :2 * tap_count * tap_count]]
  transfers between devices with their start and end apart: 1 -> 0, of which waited for: 1 -> 0; matrix products, arithmetic and copies ran while one was open for 5% -> 0% of each run, Pallas kernels for 0% -> 0%
where the time goes in v1:
time: 60.8 us; the launch traced here: 60.4 us
  Pallas kernels  52.6 us (87%)
  local copies, waits for them, and re-layouts  7.2 us (12%)
  between operations  0.68 us (1%)
    pallas_call x1, Pallas kernels, body(): pl.pallas_call(functools.partial(kernel, n_seq, n_mp), out_shape=(out, ou...  52.6 us
    unnamed x18, local copies, waits for them, and re-layouts  6.5 us

profile of v1, /device:TPU:1, one launch (start us, length us, event | category | flops | bytes accessed | tf_op | source)
XLA Modules:
  0.0 60.4 jit_solution(5563864191683142574)
XLA Ops:
  0.6 0.0 copy-start.7
  0.6 0.0 copy-start.6
  0.7 0.0 copy-start.5
  0.7 0.7 %reshape.7.gain_hbm = bf16[1,512]{1,0:T(2,128)(2,1)S(1)} reshape(bf16[512]{0:T(512)(128)(2,1)} %param.15) | data formatting | bytes 2048 | tf_op jit(solution)/shard_map/reshape | solution.py:415
  1.4 0.0 copy-done.7
  1.4 0.0 copy-done.6
  1.4 0.0 copy-done.5
  1.4 0.0 copy-start
  1.4 1.0 %copy-done = bf16[512,512]{1,0:T(8,128)(2,1)S(1)} copy-done((bf16[512,512]{1,0:T(8,128)(2,1)S(1)}, bf16[512,512]{1,0:T(8,128)(2,1)}, u32[]{:S(2)}) %copy-start) | copy-done | bytes 524312
  2.4 0.0 copy-start.1
  2.4 1.0 %copy-done.1 = bf16[512,512]{1,0:T(8,128)(2,1)S(1)} copy-done((bf16[512,512]{1,0:T(8,128)(2,1)S(1)}, bf16[512,512]{1,0:T(8,128)(2,1)}, u32[]{:S(2)}) %copy-start.1) | copy-done | bytes 524312
  3.5 0.0 copy-start.2
  3.5 1.0 %copy-done.2 = bf16[512,512]{1,0:T(8,128)(2,1)S(1)} copy-done((bf16[512,512]{1,0:T(8,128)(2,1)S(1)}, bf16[512,512]{1,0:T(8,128)(2,1)}, u32[]{:S(2)}) %copy-start.2) | copy-done | bytes 524312
  4.5 0.0 copy-start.3
  4.5 1.0 %copy-done.3 = bf16[512,512]{1,0:T(8,128)(2,1)S(1)} copy-done((bf16[512,512]{1,0:T(8,128)(2,1)S(1)}, bf16[512,512]{1,0:T(8,128)(2,1)}, u32[]{:S(2)}) %copy-start.3) | copy-done | bytes 524312
  5.5 0.0 copy-start.4
  5.5 0.7 %copy-done.4 = bf16[3,7,512]{2,1,0:T(8,128)(2,1)S(1)} copy-done((bf16[3,7,512]{2,1,0:T(8,128)(2,1)S(1)}, bf16[3,7,512]{2,1,0:T(8,128)(2,1)}, u32[]{:S(2)}) %copy-start.4) | copy-done | bytes 21528
  6.3 52.6 %shard_map.104 = (bf16[512,512]{1,0:T(8,128)(2,1)S(1)}, bf16[512,512]{1,0:T(8,128)(2,1)S(1)}) custom-call(bf16[512,512]{1,0:T(8,128)(2,1)S(1)} %copy-done, bf16[512,512]{1,0:T(8,128)(2,1)S(1)} %copy-done.1, bf16[512,512]{1,0:T(8,128)(2,1)S(1)} %copy-done.2, bf16[512,512]{1,0:T(8,128)(2,1)S(1)} %copy-done.3, bf16[3,7,512]{2,1,0:T(8,128)(2,1)S(1)} %copy-done.4, ...), custom_call_target="tpu_custom_call" | custom-call | tf_op jit(solution)/shard_map/pallas_call | solution.py:367
  58.9 0.8 %copy.13 = bf16[512,512]{1,0:T(8,128)(2,1)} copy(bf16[512,512]{1,0:T(8,128)(2,1)S(1)} %get-tuple-element.4) | data formatting | bytes 1048576
  59.6 0.8 %copy.14 = bf16[512,512]{1,0:T(8,128)(2,1)} copy(bf16[512,512]{1,0:T(8,128)(2,1)S(1)} %get-tuple-element.5) | data formatting | bytes 1048576
Async XLA Ops:
  0.6 0.7 %copy-start.7 = (s32[32]{0:T(128)S(1)}, s32[32]{0:T(128)}, u32[]{:S(2)}) copy-start(s32[32]{0:T(128)} %len_ref.1) | copy-start | bytes 388
  0.6 0.7 %copy-start.6 = (s32[32]{0:T(128)S(1)}, s32[32]{0:T(128)}, u32[]{:S(2)}) copy-start(s32[32]{0:T(128)} %pred_ref.1) | copy-start | bytes 388
  0.7 0.7 %copy-start.5 = (bf16[4,32]{1,0:T(4,128)(2,1)S(1)}, bf16[4,32]{1,0:T(4,128)(2,1)}, u32[]{:S(2)}) copy-start(bf16[4,32]{1,0:T(4,128)(2,1)} %filt_hbm.1) | copy-start | bytes 772
  1.4 1.0 %copy-start = (bf16[512,512]{1,0:T(8,128)(2,1)S(1)}, bf16[512,512]{1,0:T(8,128)(2,1)}, u32[]{:S(2)}) copy-start(bf16[512,512]{1,0:T(8,128)(2,1)} %q_hbm.1) | copy-start | bytes 1572868
  2.4 1.0 %copy-start.1 = (bf16[512,512]{1,0:T(8,128)(2,1)S(1)}, bf16[512,512]{1,0:T(8,128)(2,1)}, u32[]{:S(2)}) copy-start(bf16[512,512]{1,0:T(8,128)(2,1)} %k_hbm.1) | copy-start | bytes 1572868
  3.5 1.0 %copy-start.2 = (bf16[512,512]{1,0:T(8,128)(2,1)S(1)}, bf16[512,512]{1,0:T(8,128)(2,1)}, u32[]{:S(2)}) copy-start(bf16[512,512]{1,0:T(8,128)(2,1)} %v_hbm.1) | copy-start | bytes 1572868
  4.5 1.0 %copy-start.3 = (bf16[512,512]{1,0:T(8,128)(2,1)S(1)}, bf16[512,512]{1,0:T(8,128)(2,1)}, u32[]{:S(2)}) copy-start(bf16[512,512]{1,0:T(8,128)(2,1)} %r_hbm.1) | copy-start | bytes 1572868
  5.5 0.7 %copy-start.4 = (bf16[3,7,512]{2,1,0:T(8,128)(2,1)S(1)}, bf16[3,7,512]{2,1,0:T(8,128)(2,1)}, u32[]{:S(2)}) copy-start(bf16[3,7,512]{2,1,0:T(8,128)(2,1)} %taps_hbm.1) | copy-start | bytes 64516

commit v2 on v1

--- a/solution.py
+++ b/solution.py
@@ -1,4 +1,5 @@
 import functools
+import itertools
 
 import jax
 import jax.numpy as jnp
@@ -17,9 +18,26 @@
 GSIZE = 16
 PAD = 16
 CHUNK = 64
-SLOT = 20
+TILE = 16
+EXTRA = 4
 F32 = jnp.float32
 BF16 = jnp.bfloat16
+
+
+def farthest_first(sizes, hops):
+    offsets = list(itertools.product(*(range(size) for size in sizes)))[1:]
+    way = lambda offset: sum(
+        min(step, size - step) * hop for step, size, hop in zip(offset, sizes, hops)
+    )
+    return sorted(offsets, key=way, reverse=True)
+
+
+def moved(index, sizes, offset):
+    result, weight = 0, 1
+    for size, step in zip(reversed(sizes), reversed(offset)):
+        result = result + weight * lax.rem(lax.rem(index // weight, size) + step, size)
+        weight *= size
+    return result
 
 
 def kernel(
@@ -50,6 +68,10 @@
     recv,
     fwd,
     fin,
+    xmsg,
+    xrecv,
+    xfwd,
+    xfin,
     rows_f,
     toep,
     flipped,
@@ -67,26 +89,13 @@
     recv2,
     send3,
     recv3,
+    xsend1,
+    xrecv1,
+    xsend2,
+    xrecv2,
 ):
     me = lax.axis_index("seq")
     mine = lax.axis_index("mp")
-
-    barrier = pltpu.get_barrier_semaphore()
-
-    def hello_seq(d, _):
-        pl.semaphore_signal(
-            barrier, inc=1, device_id={"seq": lax.rem(me + d, n_seq)}, device_id_type=MESH
-        )
-        return 0
-
-    def hello_mp(d, _):
-        pl.semaphore_signal(
-            barrier, inc=1, device_id={"mp": lax.rem(mine + d, n_mp)}, device_id_type=MESH
-        )
-        return 0
-
-    lax.fori_loop(1, n_seq, hello_seq, 0)
-    lax.fori_loop(1, n_mp, hello_mp, 0)
 
     body = pl.ds(PAD, ROWS)
     loads = [
@@ -100,6 +109,30 @@
     ]
     for load in loads:
         load.start()
+    seq_parts, mp_parts = (n_seq // 2, 2), ((n_mp // 4, 2, 2) if n_mp % 4 == 0 else (n_mp,))
+    seq_peers = [
+        moved(me, seq_parts, offset) for offset in farthest_first(seq_parts, (1, 1))
+    ]
+    mp_peers = [
+        moved(mine, mp_parts, offset)
+        for offset in farthest_first(mp_parts, (2, 4, 1) if n_mp % 4 == 0 else (1,))
+    ]
+    barrier = pltpu.get_barrier_semaphore()
+    for peer in seq_peers:
+        pl.semaphore_signal(barrier, inc=1, device_id={"seq": peer}, device_id_type=MESH)
+    for peer in mp_peers:
+        pl.semaphore_signal(barrier, inc=1, device_id={"mp": peer}, device_id_type=MESH)
+
+    def spread_out(source, landing, send_sem, recv_sem, peer):
+        pltpu.make_async_remote_copy(
+            src_ref=source,
+            dst_ref=landing.at[me],
+            send_sem=send_sem,
+            recv_sem=recv_sem,
+            device_id={"seq": peer},
+            device_id_type=MESH,
+        ).start()
+
     for ref in (qbuf, kbuf, vbuf):
         ref[0:PAD, :] = jnp.zeros((PAD, WIDTH), BF16)
     for load in loads[:4]:
@@ -130,10 +163,15 @@
             value = product(start, CHUNK, lanes)
             mix[pl.ds(TAPS + start, CHUNK), lanes] = value
             for a in range(CHUNK // 16):
-                msg[(c * (CHUNK // 16) + a) * tiles + b, 0:16, :] = value[16 * a : 16 * a + 16]
+                msg[(c * (CHUNK // 16) + a) * tiles + b] = value[16 * a : 16 * a + 16]
         return 0
 
     lax.fori_loop(0, tail_chunks, tail_step, 0)
+
+    pl.semaphore_wait(barrier, n_seq + n_mp - 2)
+    for peer in seq_peers:
+        spread_out(msg.at[peer], recv, send1, recv1, peer)
+    recv[me] = msg[me]
 
     loads[4].wait()
     for i, ref in enumerate((qbuf, kbuf, vbuf)):
@@ -147,27 +185,13 @@
         rows_f[pl.ds(4 * b + 3, 8, stride=16), :] = jnp.broadcast_to(row, (8, LANES))
 
     def pack(p, _):
-        msg[p, 16:20, :] = rows_f[pl.ds(pl.multiple_of(4 * p, 4), 4), :].astype(BF16)
+        xmsg[p] = rows_f[pl.ds(pl.multiple_of(4 * p, 4), 4), :].astype(BF16)
         return 0
 
     lax.fori_loop(0, n_seq, pack, 0)
-    recv[me] = msg[me]
-
-    pl.semaphore_wait(barrier, n_seq + n_mp - 2)
-
-    def scatter(d, _):
-        p = lax.rem(me + d, n_seq)
-        pltpu.make_async_remote_copy(
-            src_ref=msg.at[p],
-            dst_ref=recv.at[me],
-            send_sem=send1,
-            recv_sem=recv1,
-            device_id={"seq": p},
-            device_id_type=MESH,
-        ).start()
-        return 0
-
-    lax.fori_loop(1, n_seq, scatter, 0)
+    for peer in seq_peers:
+        spread_out(xmsg.at[peer], xrecv, xsend1, xrecv1, peer)
+    xrecv[me] = xmsg[me]
 
     def rest_step(c, _):
         start = pl.multiple_of(c * CHUNK, CHUNK)
@@ -191,30 +215,19 @@
     others = pl.ds(0, n_seq - 1)
     pltpu.make_async_copy(recv.at[others], recv.at[others], recv1).wait()
 
-    def forward(i):
-        source = pred_ref[i]
-        keep = (source >= 0).astype(F32)
-        piece = recv[jnp.maximum(source, 0)]
-        return (piece.astype(F32) * keep).astype(BF16)
-
-    def route(d, _):
-        i = lax.rem(me + d, n_seq)
-        fwd[i] = forward(i)
-        pltpu.make_async_remote_copy(
-            src_ref=fwd.at[i],
-            dst_ref=fin.at[me],
-            send_sem=send2,
-            recv_sem=recv2,
-            device_id={"seq": i},
-            device_id_type=MESH,
-        ).start()
-        return 0
-
-    lax.fori_loop(1, n_seq, route, 0)
-    fin[me] = forward(me)
+    for peer in seq_peers:
+        fwd[peer] = recv[jnp.maximum(pred_ref[peer], 0)]
+        spread_out(fwd.at[peer], fin, send2, recv2, peer)
+    fin[me] = recv[jnp.maximum(pred_ref[me], 0)]
+
+    pltpu.make_async_copy(xrecv.at[others], xrecv.at[others], xrecv1).wait()
+    for peer in seq_peers:
+        xfwd[peer] = xrecv[jnp.maximum(pred_ref[peer], 0)]
+        spread_out(xfwd.at[peer], xfin, xsend2, xrecv2, peer)
+    xfin[me] = xrecv[jnp.maximum(pred_ref[me], 0)]
 
     def unpack_recv(p, _):
-        rows_f[pl.ds(pl.multiple_of(4 * p, 4), 4), :] = recv[p, 16:20, :].astype(F32)
+        rows_f[pl.ds(pl.multiple_of(4 * p, 4), 4), :] = xrecv[p].astype(F32)
         return 0
 
     lax.fori_loop(0, n_seq, unpack_recv, 0)
@@ -287,14 +300,18 @@
 
     pltpu.make_async_copy(fin.at[others], fin.at[others], recv2).wait()
 
+    pltpu.make_async_copy(xfin.at[others], xfin.at[others], xrecv2).wait()
+    keep = (pred_ref[me] >= 0).astype(F32)
+
     def unpack_fin(p, _):
-        rows_f[pl.ds(pl.multiple_of(4 * p, 4), 4), :] = fin[p, 16:20, :].astype(F32)
+        rows_f[pl.ds(pl.multiple_of(4 * p, 4), 4), :] = xfin[p].astype(F32) * keep
         return 0
 
     lax.fori_loop(0, n_seq, unpack_fin, 0)
     for a in range(TAPS // 16):
         for b in range(tiles):
-            mix[16 * a : 16 * a + 16, b * LANES : (b + 1) * LANES] = fin[a * tiles + b, 0:16, :]
+            piece = (fin[a * tiles + b].astype(F32) * keep).astype(BF16)
+            mix[16 * a : 16 * a + 16, b * LANES : (b + 1) * LANES] = piece
     for i, ref in enumerate((qbuf, kbuf, vbuf)):
         for b in range(tiles):
             head = rows_f[pl.ds(4 * b + i, 8, stride=16), :]
@@ -315,24 +332,21 @@
         part[:, span] = jnp.sum(squares[span, :].T, axis=0, keepdims=True)
     parts[mine] = part[...]
 
-    def share_part(d, _):
+    for peer in mp_peers:
         pltpu.make_async_remote_copy(
             src_ref=part,
             dst_ref=parts.at[mine],
             send_sem=send3,
             recv_sem=recv3,
-            device_id={"mp": lax.rem(mine + d, n_mp)},
+            device_id={"mp": peer},
             device_id_type=MESH,
         ).start()
-        return 0
-
-    lax.fori_loop(1, n_mp, share_part, 0)
     if n_mp > 1:
         peers = pl.ds(0, n_mp - 1)
         pltpu.make_async_copy(parts.at[peers], parts.at[peers], recv3).wait()
     total = jnp.sum(parts[...], axis=0)
     scale = lax.rsqrt(total / (WIDTH * n_mp) + EPSILON)
-    gain = gainb[...].astype(F32)
+    gain = gainb[...].astype(F32).reshape(1, WIDTH)
     for blk in range(ROWS // TAPS):
         span = slice(blk * TAPS, (blk + 1) * TAPS)
         column = jnp.broadcast_to(scale[:, span], (TAPS, LANES)).T
@@ -352,6 +366,8 @@
 
     pltpu.make_async_copy(msg.at[others], msg.at[others], send1).wait()
     pltpu.make_async_copy(fwd.at[others], fwd.at[others], send2).wait()
+    pltpu.make_async_copy(xmsg.at[others], xmsg.at[others], xsend1).wait()
+    pltpu.make_async_copy(xfwd.at[others], xfwd.at[others], xsend2).wait()
     if n_mp > 1:
         pltpu.make_async_copy(parts.at[peers], parts.at[peers], send3).wait()
     for store in stores:
@@ -359,9 +375,9 @@
 
 
 def body(n_seq, n_mp, queries, keys_in, values_in, residual, short_taps, mr_filter, norm_gain, predecessor, stretch_lengths):
-    whole = pl.BlockSpec(memory_space=pl.ANY)
+    whole = pl.BlockSpec(memory_space=pltpu.HBM)
     scalars = pl.BlockSpec(memory_space=pltpu.SMEM)
-    slots = (n_seq, SLOT, LANES)
+    slots, extras = (n_seq, TILE, LANES), (n_seq, EXTRA, LANES)
     share, groups = mr_filter.shape
     out = jax.ShapeDtypeStruct((ROWS, WIDTH), BF16)
     return pl.pallas_call(
@@ -376,14 +392,12 @@
             pltpu.VMEM((ROWS, WIDTH), BF16),
             pltpu.VMEM((3, SHORT, WIDTH), BF16),
             pltpu.VMEM((share, groups), BF16),
-            pltpu.VMEM((1, WIDTH), BF16),
+            pltpu.VMEM((WIDTH,), BF16),
             pltpu.VMEM((24, WIDTH), F32),
             pltpu.VMEM((ROWS, WIDTH), F32),
             pltpu.VMEM((TAPS + ROWS, WIDTH), BF16),
-            pltpu.VMEM(slots, BF16),
-            pltpu.VMEM(slots, BF16),
-            pltpu.VMEM(slots, BF16),
-            pltpu.VMEM(slots, BF16),
+            *[pltpu.VMEM(slots, BF16)] * 4,
+            *[pltpu.VMEM(extras, BF16)] * 4,
             pltpu.VMEM((LANES, LANES), F32),
             pltpu.VMEM((groups * TAPS, 2 * TAPS), BF16),
             pltpu.VMEM((groups, LANES), F32),
@@ -395,15 +409,10 @@
             pltpu.VMEM((n_mp, 1, ROWS), F32),
             pltpu.SemaphoreType.DMA((7,)),
             pltpu.SemaphoreType.DMA((6,)),
-            pltpu.SemaphoreType.DMA,
-            pltpu.SemaphoreType.DMA,
-            pltpu.SemaphoreType.DMA,
-            pltpu.SemaphoreType.DMA,
-            pltpu.SemaphoreType.DMA,
-            pltpu.SemaphoreType.DMA,
+            *[pltpu.SemaphoreType.DMA] * 10,
         ],
         compiler_params=pltpu.CompilerParams(
-            collective_id=0, has_side_effects=True, vmem_limit_bytes=40 * 1024 * 1024
+            collective_id=0, has_side_effects=True, vmem_limit_bytes=58 * 1024 * 1024
         ),
     )(
         queries,
@@ -412,7 +421,7 @@
         residual,
         short_taps,
         mr_filter,
-        norm_gain.reshape(1, WIDTH),
+        norm_gain,
         predecessor,
         stretch_lengths,
     )

time: 60.8 us -> 50.9 us (0.84)
  Pallas kernels: 52.6 us -> 47.4 us
  local copies, waits for them, and re-layouts: 7.2 us -> 2.72 us
    pallas_call x1, Pallas kernels: 52.6 us -> 47.4 us  [body(): pl.pallas_call(functools.partial(kernel, n_seq, n_mp), out_shape=(out, ou...]
    unnamed x18 -> x4, local copies, waits for them, and re-layouts: 6.5 us -> 2.72 us
    reshape x1 -> x0, local copies, waits for them, and re-layouts: 0.7 us -> none  [body(): norm_gain.reshape(1, WIDTH)]
where the time goes in v2:
time: 50.9 us; the launch traced here: 50.7 us
  Pallas kernels  47.4 us (93%)
  local copies, waits for them, and re-layouts  2.72 us (5%)
  between operations  0.65 us (1%)
    pallas_call x1, Pallas kernels, body(): pl.pallas_call(functools.partial(kernel, n_seq, n_mp), out_shape=(out, ou...  47.4 us
    unnamed x4, local copies, waits for them, and re-layouts  2.72 us

profile of v2, /device:TPU:1, one launch (start us, length us, event | category | flops | bytes accessed | tf_op | source)
XLA Modules:
  0.0 50.7 jit_solution(6614681833578218452)
XLA Ops:
  0.6 47.4 %shard_map.104 = (bf16[512,512]{1,0:T(8,128)(2,1)}, bf16[512,512]{1,0:T(8,128)(2,1)}) custom-call(bf16[512,512]{1,0:T(8,128)(2,1)} %q_hbm.1, bf16[512,512]{1,0:T(8,128)(2,1)} %k_hbm.1, bf16[512,512]{1,0:T(8,128)(2,1)} %v_hbm.1, bf16[512,512]{1,0:T(8,128)(2,1)} %r_hbm.1, bf16[3,7,512]{2,1,0:T(8,128)(2,1)} %taps_hbm.1, bf16[4,32]{1,0:T(4,128)(2,1)} %filt_hbm.1, ...), custom_call_target="tpu_custom_call" | custom-call | tf_op jit(solution)/shard_map/pallas_call | solution.py:383
  48.0 0.0 copy-start
  48.0 1.9 %copy.13 = bf16[512,512]{1,0:T(8,128)(2,1)} copy(bf16[512,512]{1,0:T(8,128)(2,1)} %get-tuple-element.4) | data formatting | bytes 1048576
  49.9 0.0 copy-done
  50.0 0.8 %copy.14 = bf16[512,512]{1,0:T(8,128)(2,1)} copy(bf16[512,512]{1,0:T(8,128)(2,1)S(1)} %copy-done) | data formatting | bytes 1048576
Async XLA Ops:
  48.0 1.9 %copy-start = (bf16[512,512]{1,0:T(8,128)(2,1)S(1)}, bf16[512,512]{1,0:T(8,128)(2,1)}, u32[]{:S(2)}) copy-start(bf16[512,512]{1,0:T(8,128)(2,1)} %get-tuple-element.5) | copy-start | bytes 1572868

commit v3 on v2

--- a/solution.py
+++ b/solution.py
@@ -20,6 +20,7 @@
 CHUNK = 64
 TILE = 16
 EXTRA = 4
+LIMIT = 58 * 1024 * 1024
 F32 = jnp.float32
 BF16 = jnp.bfloat16
 
@@ -52,15 +53,15 @@
     gain_hbm,
     pred_ref,
     len_ref,
-    mixed_hbm,
-    normed_hbm,
+    mixed_v,
+    rbuf,
+    scale_ref,
+    gain_ref,
     qbuf,
     kbuf,
     vbuf,
-    rbuf,
     tapsb,
     filtb,
-    gainb,
     taps,
     qfeat,
     mix,
@@ -75,14 +76,10 @@
     rows_f,
     toep,
     flipped,
-    summed,
     squares,
-    mixed_v,
-    normed_v,
     part,
     parts,
     load_sem,
-    store_sem,
     send1,
     recv1,
     send2,
@@ -97,15 +94,25 @@
     me = lax.axis_index("seq")
     mine = lax.axis_index("mp")
 
-    body = pl.ds(PAD, ROWS)
+    last = TAPS + PAD
+    early, late = pl.ds(0, ROWS - last), pl.ds(ROWS - last, last)
+    late_body, early_body = pl.ds(PAD + ROWS - last, last), pl.ds(PAD, ROWS - last)
+    whole_body = pl.ds(PAD, ROWS)
     loads = [
-        pltpu.make_async_copy(k_hbm, kbuf.at[body], load_sem.at[0]),
-        pltpu.make_async_copy(v_hbm, vbuf.at[body], load_sem.at[1]),
-        pltpu.make_async_copy(taps_hbm, tapsb, load_sem.at[2]),
-        pltpu.make_async_copy(filt_hbm, filtb, load_sem.at[3]),
-        pltpu.make_async_copy(q_hbm, qbuf.at[body], load_sem.at[4]),
-        pltpu.make_async_copy(r_hbm, rbuf, load_sem.at[5]),
-        pltpu.make_async_copy(gain_hbm, gainb, load_sem.at[6]),
+        pltpu.make_async_copy(source, target, load_sem.at[i])
+        for i, (source, target) in enumerate(
+            (
+                (taps_hbm, tapsb),
+                (k_hbm.at[late], kbuf.at[late_body]),
+                (v_hbm.at[late], vbuf.at[late_body]),
+                (q_hbm, qbuf.at[whole_body]),
+                (filt_hbm, filtb),
+                (k_hbm.at[early], kbuf.at[early_body]),
+                (v_hbm.at[early], vbuf.at[early_body]),
+                (r_hbm, rbuf),
+                (gain_hbm, gain_ref),
+            )
+        )
     ]
     for load in loads:
         load.start()
@@ -135,7 +142,7 @@
 
     for ref in (qbuf, kbuf, vbuf):
         ref[0:PAD, :] = jnp.zeros((PAD, WIDTH), BF16)
-    for load in loads[:4]:
+    for load in loads[:3]:
         load.wait()
     for branch in range(3):
         taps[8 * branch : 8 * branch + SHORT, :] = tapsb[branch].astype(F32)
@@ -173,6 +180,7 @@
         spread_out(msg.at[peer], recv, send1, recv1, peer)
     recv[me] = msg[me]
 
+    loads[3].wait()
     loads[4].wait()
     for i, ref in enumerate((qbuf, kbuf, vbuf)):
         tail = ref[PAD + ROWS - 16 : PAD + ROWS, :].astype(F32)[8:]
@@ -193,6 +201,8 @@
         spread_out(xmsg.at[peer], xrecv, xsend1, xrecv1, peer)
     xrecv[me] = xmsg[me]
 
+    loads[5].wait()
+    loads[6].wait()
     def rest_step(c, _):
         start = pl.multiple_of(c * CHUNK, CHUNK)
         for b in range(tiles):
@@ -257,8 +267,8 @@
     lax.fori_loop(0, groups, toeplitz, 0)
 
     length = len_ref[me]
-    loads[5].wait()
-    loads[6].wait()
+    loads[7].wait()
+    loads[8].wait()
     in_tile = LANES // GSIZE
     lane_group = lax.broadcasted_iota(jnp.int32, (TAPS, LANES), 1) // GSIZE
 
@@ -284,19 +294,12 @@
                 mixed = jnp.where(valid, qfeat[span, lanes] * out, 0.0).astype(BF16)
                 mixed_v[span, lanes] = mixed
                 total = rbuf[span, lanes].astype(F32) + mixed.astype(F32)
-                summed[span, lanes] = total
                 squares[span, :] = squares[span, :] + total * total
             return 0
 
         lax.fori_loop(0, tiles, step, 0)
 
-    def store_pair(pair, sem):
-        span = pl.ds(pair[0] * TAPS, len(pair) * TAPS)
-        return pltpu.make_async_copy(mixed_v.at[span], mixed_hbm.at[span], sem)
-
     convolve((2, 3))
-    stores = [store_pair((2, 3), store_sem.at[0])]
-    stores[0].start()
 
     pltpu.make_async_copy(fin.at[others], fin.at[others], recv2).wait()
 
@@ -324,8 +327,6 @@
         qfeat[0:16, lanes] = featurize(qbuf, 0, 0, 16, lanes)
 
     convolve((0, 1))
-    stores.append(store_pair((0, 1), store_sem.at[1]))
-    stores[1].start()
 
     for blk in range(ROWS // TAPS):
         span = slice(blk * TAPS, (blk + 1) * TAPS)
@@ -345,24 +346,9 @@
         peers = pl.ds(0, n_mp - 1)
         pltpu.make_async_copy(parts.at[peers], parts.at[peers], recv3).wait()
     total = jnp.sum(parts[...], axis=0)
+    token = lax.broadcasted_iota(jnp.int32, (1, ROWS), 1)
     scale = lax.rsqrt(total / (WIDTH * n_mp) + EPSILON)
-    gain = gainb[...].astype(F32).reshape(1, WIDTH)
-    for blk in range(ROWS // TAPS):
-        span = slice(blk * TAPS, (blk + 1) * TAPS)
-        column = jnp.broadcast_to(scale[:, span], (TAPS, LANES)).T
-        valid = (lax.broadcasted_iota(jnp.int32, (TAPS, LANES), 0) + blk * TAPS) < length
-        for b in range(tiles):
-            lanes = slice(b * LANES, (b + 1) * LANES)
-            normed_v[span, lanes] = jnp.where(
-                valid, summed[span, lanes] * column * gain[:, lanes], 0.0
-            ).astype(BF16)
-        part_rows = pl.ds(blk * TAPS, TAPS)
-        stores.append(
-            pltpu.make_async_copy(
-                normed_v.at[part_rows], normed_hbm.at[part_rows], store_sem.at[2 + blk]
-            )
-        )
-        stores[-1].start()
+    scale_ref[...] = jnp.where(token < length, scale, 0.0)
 
     pltpu.make_async_copy(msg.at[others], msg.at[others], send1).wait()
     pltpu.make_async_copy(fwd.at[others], fwd.at[others], send2).wait()
@@ -370,6 +356,23 @@
     pltpu.make_async_copy(xfwd.at[others], xfwd.at[others], xsend2).wait()
     if n_mp > 1:
         pltpu.make_async_copy(parts.at[peers], parts.at[peers], send3).wait()
+
+
+def finish(gated, resid, scale_ref, gain_ref, mixed_hbm, normed_hbm, normed, sem):
+    stores = [pltpu.make_async_copy(gated, mixed_hbm, sem.at[0])]
+    stores[0].start()
+    gain = gain_ref[...].astype(F32).reshape(1, WIDTH)
+    for blk in range(ROWS // TAPS):
+        rows = pl.ds(blk * TAPS, TAPS)
+        factor = jnp.broadcast_to(scale_ref[:, blk * TAPS : (blk + 1) * TAPS], (TAPS, LANES)).T
+        for b in range(WIDTH // LANES):
+            lanes = slice(b * LANES, (b + 1) * LANES)
+            total = resid[rows, lanes].astype(F32) + gated[rows, lanes].astype(F32)
+            normed[rows, lanes] = (total * factor * gain[:, lanes]).astype(BF16)
+        stores.append(
+            pltpu.make_async_copy(normed.at[rows], normed_hbm.at[rows], sem.at[1 + blk])
+        )
+        stores[-1].start()
     for store in stores:
         store.wait()
 
@@ -380,19 +383,18 @@
     slots, extras = (n_seq, TILE, LANES), (n_seq, EXTRA, LANES)
     share, groups = mr_filter.shape
     out = jax.ShapeDtypeStruct((ROWS, WIDTH), BF16)
-    return pl.pallas_call(
+    row = pl.BlockSpec(memory_space=pltpu.VMEM)
+    gated, resid, scale, gain = pl.pallas_call(
         functools.partial(kernel, n_seq, n_mp),
-        out_shape=(out, out),
+        out_shape=(pltpu.VMEM((ROWS, WIDTH), BF16), pltpu.VMEM((ROWS, WIDTH), BF16), pltpu.VMEM((1, ROWS), F32), pltpu.VMEM((WIDTH,), BF16)),
         in_specs=[whole] * 7 + [scalars] * 2,
-        out_specs=(whole, whole),
+        out_specs=(row, row, row, row),
         scratch_shapes=[
             pltpu.VMEM((PAD + ROWS, WIDTH), BF16),
             pltpu.VMEM((PAD + ROWS, WIDTH), BF16),
             pltpu.VMEM((PAD + ROWS, WIDTH), BF16),
-            pltpu.VMEM((ROWS, WIDTH), BF16),
             pltpu.VMEM((3, SHORT, WIDTH), BF16),
             pltpu.VMEM((share, groups), BF16),
-            pltpu.VMEM((WIDTH,), BF16),
             pltpu.VMEM((24, WIDTH), F32),
             pltpu.VMEM((ROWS, WIDTH), F32),
             pltpu.VMEM((TAPS + ROWS, WIDTH), BF16),
@@ -401,18 +403,14 @@
             pltpu.VMEM((LANES, LANES), F32),
             pltpu.VMEM((groups * TAPS, 2 * TAPS), BF16),
             pltpu.VMEM((groups, LANES), F32),
-            pltpu.VMEM((ROWS, WIDTH), F32),
             pltpu.VMEM((ROWS, LANES), F32),
-            pltpu.VMEM((ROWS, WIDTH), BF16),
-            pltpu.VMEM((ROWS, WIDTH), BF16),
             pltpu.VMEM((1, ROWS), F32),
             pltpu.VMEM((n_mp, 1, ROWS), F32),
-            pltpu.SemaphoreType.DMA((7,)),
-            pltpu.SemaphoreType.DMA((6,)),
+            pltpu.SemaphoreType.DMA((9,)),
             *[pltpu.SemaphoreType.DMA] * 10,
         ],
         compiler_params=pltpu.CompilerParams(
-            collective_id=0, has_side_effects=True, vmem_limit_bytes=58 * 1024 * 1024
+            collective_id=0, has_side_effects=True, vmem_limit_bytes=LIMIT
         ),
     )(
         queries,
@@ -425,6 +423,17 @@
         predecessor,
         stretch_lengths,
     )
+    return pl.pallas_call(
+        finish,
+        out_shape=(out, out),
+        in_specs=[row, row, row, row],
+        out_specs=(whole, whole),
+        scratch_shapes=[
+            pltpu.VMEM((ROWS, WIDTH), BF16),
+            pltpu.SemaphoreType.DMA((1 + ROWS // TAPS,)),
+        ],
+        compiler_params=pltpu.CompilerParams(vmem_limit_bytes=16 * 1024 * 1024),
+    )(gated, resid, scale, gain)
 
 
 def solution(mesh):

time: 50.9 us -> 48.2 us (0.947)
  local copies, waits for them, and re-layouts: 2.72 us -> 0 us
    unnamed x4 -> x0, local copies, waits for them, and re-layouts: 2.72 us -> none
    pallas_call x1 -> x2, Pallas kernels: 47.4 us -> 47.4 us  [the longest x1 46.4 us: body(): pl.pallas_call(functools.partial(kernel, n_seq, n_mp), out_shape=(pltpu.V...]
where the time goes in v3:
time: 48.2 us; the launch traced here: 48 us
  Pallas kernels  47.4 us (98%)
  between operations  0.64 us (1%)
    pallas_call x1, Pallas kernels, body(): pl.pallas_call(functools.partial(kernel, n_seq, n_mp), out_shape=(pltpu.V...  46.4 us
    pallas_call x1, Pallas kernels, body(): pl.pallas_call(finish, out_shape=(out, out), in_specs=[row, row, row, row...  1 us

profile of v3, /device:TPU:1, one launch (start us, length us, event | category | flops | bytes accessed | tf_op | source)
XLA Modules:
  0.0 48.0 jit_solution(3610353033584886757)
XLA Ops:
  0.6 46.4 %shard_map.104 = (bf16[512,512]{1,0:T(8,128)(2,1)S(1)}, bf16[512,512]{1,0:T(8,128)(2,1)S(1)}, f32[1,512]{1,0:T(1,128)S(1)}, bf16[512]{0:T(512)(128)(2,1)S(1)}) custom-call(bf16[512,512]{1,0:T(8,128)(2,1)} %q_hbm.1, bf16[512,512]{1,0:T(8,128)(2,1)} %k_hbm.1, bf16[512,512]{1,0:T(8,128)(2,1)} %v_hbm.1, bf16[512,512]{1,0:T(8,128)(2,1)} %r_hbm.1, ...), custom_call_target="tpu_custom_call" | custom-call | tf_op jit(solution)/shard_map/pallas_call | solution.py:387
  47.0 1.0 %shard_map.105 = (bf16[512,512]{1,0:T(8,128)(2,1)}, bf16[512,512]{1,0:T(8,128)(2,1)}) custom-call(bf16[512,512]{1,0:T(8,128)(2,1)S(1)} %get-tuple-element.6.gated, bf16[512,512]{1,0:T(8,128)(2,1)S(1)} %get-tuple-element.7.resid, f32[1,512]{1,0:T(1,128)S(1)} %get-tuple-element.8.scale_ref, bf16[512]{0:T(512)(128)(2,1)S(1)} %get-tuple-element.9.gain_ref), custom_call_target="tpu_custom_call" | custom-call | tf_op jit(solution)/shard_map/pallas_call | solution.py:426

commit v4 on v3

--- a/solution.py
+++ b/solution.py
@@ -18,8 +18,8 @@
 GSIZE = 16
 PAD = 16
 CHUNK = 64
+QUAD = 4
 TILE = 16
-EXTRA = 4
 LIMIT = 58 * 1024 * 1024
 F32 = jnp.float32
 BF16 = jnp.bfloat16
@@ -69,10 +69,6 @@
     recv,
     fwd,
     fin,
-    xmsg,
-    xrecv,
-    xfwd,
-    xfin,
     rows_f,
     toep,
     flipped,
@@ -86,10 +82,6 @@
     recv2,
     send3,
     recv3,
-    xsend1,
-    xrecv1,
-    xsend2,
-    xrecv2,
 ):
     me = lax.axis_index("seq")
     mine = lax.axis_index("mp")
@@ -169,16 +161,14 @@
             start = pl.multiple_of(ROWS - TAPS + c * CHUNK, CHUNK)
             value = product(start, CHUNK, lanes)
             mix[pl.ds(TAPS + start, CHUNK), lanes] = value
-            for a in range(CHUNK // 16):
-                msg[(c * (CHUNK // 16) + a) * tiles + b] = value[16 * a : 16 * a + 16]
+            for a in range(CHUNK // TILE):
+                p = (c * (CHUNK // TILE) + a) * tiles + b
+                for i in range(TILE // QUAD):
+                    first = TILE * a + QUAD * i
+                    msg[p, i] = value[first : first + QUAD]
         return 0
 
     lax.fori_loop(0, tail_chunks, tail_step, 0)
-
-    pl.semaphore_wait(barrier, n_seq + n_mp - 2)
-    for peer in seq_peers:
-        spread_out(msg.at[peer], recv, send1, recv1, peer)
-    recv[me] = msg[me]
 
     loads[3].wait()
     loads[4].wait()
@@ -193,13 +183,14 @@
         rows_f[pl.ds(4 * b + 3, 8, stride=16), :] = jnp.broadcast_to(row, (8, LANES))
 
     def pack(p, _):
-        xmsg[p] = rows_f[pl.ds(pl.multiple_of(4 * p, 4), 4), :].astype(BF16)
+        msg[p, TILE // QUAD] = rows_f[pl.ds(pl.multiple_of(4 * p, 4), 4), :].astype(BF16)
         return 0
 
     lax.fori_loop(0, n_seq, pack, 0)
+    pl.semaphore_wait(barrier, n_seq + n_mp - 2)
     for peer in seq_peers:
-        spread_out(xmsg.at[peer], xrecv, xsend1, xrecv1, peer)
-    xrecv[me] = xmsg[me]
+        spread_out(msg.at[peer], recv, send1, recv1, peer)
+    recv[me] = msg[me]
 
     loads[5].wait()
     loads[6].wait()
@@ -230,14 +221,8 @@
         spread_out(fwd.at[peer], fin, send2, recv2, peer)
     fin[me] = recv[jnp.maximum(pred_ref[me], 0)]
 
-    pltpu.make_async_copy(xrecv.at[others], xrecv.at[others], xrecv1).wait()
-    for peer in seq_peers:
-        xfwd[peer] = xrecv[jnp.maximum(pred_ref[peer], 0)]
-        spread_out(xfwd.at[peer], xfin, xsend2, xrecv2, peer)
-    xfin[me] = xrecv[jnp.maximum(pred_ref[me], 0)]
-
     def unpack_recv(p, _):
-        rows_f[pl.ds(pl.multiple_of(4 * p, 4), 4), :] = xrecv[p].astype(F32)
+        rows_f[pl.ds(pl.multiple_of(4 * p, 4), 4), :] = recv[p, TILE // QUAD].astype(F32)
         return 0
 
     lax.fori_loop(0, n_seq, unpack_recv, 0)
@@ -303,18 +288,20 @@
 
     pltpu.make_async_copy(fin.at[others], fin.at[others], recv2).wait()
 
-    pltpu.make_async_copy(xfin.at[others], xfin.at[others], xrecv2).wait()
     keep = (pred_ref[me] >= 0).astype(F32)
 
     def unpack_fin(p, _):
-        rows_f[pl.ds(pl.multiple_of(4 * p, 4), 4), :] = xfin[p].astype(F32) * keep
+        rows_f[pl.ds(pl.multiple_of(4 * p, 4), 4), :] = fin[p, TILE // QUAD].astype(F32) * keep
         return 0
 
     lax.fori_loop(0, n_seq, unpack_fin, 0)
     for a in range(TAPS // 16):
         for b in range(tiles):
-            piece = (fin[a * tiles + b].astype(F32) * keep).astype(BF16)
-            mix[16 * a : 16 * a + 16, b * LANES : (b + 1) * LANES] = piece
+            lanes = slice(b * LANES, (b + 1) * LANES)
+            for i in range(TILE // QUAD):
+                first = TILE * a + QUAD * i
+                mix[first : first + QUAD, lanes] = fin[a * tiles + b, i]
+    mix[0:TAPS, :] = (mix[0:TAPS, :].astype(F32) * keep).astype(BF16)
     for i, ref in enumerate((qbuf, kbuf, vbuf)):
         for b in range(tiles):
             head = rows_f[pl.ds(4 * b + i, 8, stride=16), :]
@@ -352,8 +339,6 @@
 
     pltpu.make_async_copy(msg.at[others], msg.at[others], send1).wait()
     pltpu.make_async_copy(fwd.at[others], fwd.at[others], send2).wait()
-    pltpu.make_async_copy(xmsg.at[others], xmsg.at[others], xsend1).wait()
-    pltpu.make_async_copy(xfwd.at[others], xfwd.at[others], xsend2).wait()
     if n_mp > 1:
         pltpu.make_async_copy(parts.at[peers], parts.at[peers], send3).wait()
 
@@ -380,7 +365,7 @@
 def body(n_seq, n_mp, queries, keys_in, values_in, residual, short_taps, mr_filter, norm_gain, predecessor, stretch_lengths):
     whole = pl.BlockSpec(memory_space=pltpu.HBM)
     scalars = pl.BlockSpec(memory_space=pltpu.SMEM)
-    slots, extras = (n_seq, TILE, LANES), (n_seq, EXTRA, LANES)
+    slots = (n_seq, TILE // QUAD + 1, QUAD, LANES)
     share, groups = mr_filter.shape
     out = jax.ShapeDtypeStruct((ROWS, WIDTH), BF16)
     row = pl.BlockSpec(memory_space=pltpu.VMEM)
@@ -399,7 +384,6 @@
             pltpu.VMEM((ROWS, WIDTH), F32),
             pltpu.VMEM((TAPS + ROWS, WIDTH), BF16),
             *[pltpu.VMEM(slots, BF16)] * 4,
-            *[pltpu.VMEM(extras, BF16)] * 4,
             pltpu.VMEM((LANES, LANES), F32),
             pltpu.VMEM((groups * TAPS, 2 * TAPS), BF16),
             pltpu.VMEM((groups, LANES), F32),
@@ -407,7 +391,7 @@
             pltpu.VMEM((1, ROWS), F32),
             pltpu.VMEM((n_mp, 1, ROWS), F32),
             pltpu.SemaphoreType.DMA((9,)),
-            *[pltpu.SemaphoreType.DMA] * 10,
+            *[pltpu.SemaphoreType.DMA] * 6,
         ],
         compiler_params=pltpu.CompilerParams(
             collective_id=0, has_side_effects=True, vmem_limit_bytes=LIMIT

time: 48.2 us -> 46.8 us (0.971)
  Pallas kernels: 47.4 us -> 46 us
    pallas_call x1, Pallas kernels: 46.4 us -> 45 us  [body(): pl.pallas_call(functools.partial(kernel, n_seq, n_mp), out_shape=(pltpu.V...]
where the time goes in v4:
time: 46.8 us; the launch traced here: 46.6 us
  Pallas kernels  46 us (98%)
  between operations  0.64 us (1%)
    pallas_call x1, Pallas kernels, body(): pl.pallas_call(functools.partial(kernel, n_seq, n_mp), out_shape=(pltpu.V...  45 us
    pallas_call x1, Pallas kernels, body(): pl.pallas_call(finish, out_shape=(out, out), in_specs=[row, row, row, row...  1 us

profile of v4, /device:TPU:1, one launch (start us, length us, event | category | flops | bytes accessed | tf_op | source)
XLA Modules:
  0.0 46.6 jit_solution(3370642861181156393)
XLA Ops:
  0.6 45.0 %shard_map.104 = (bf16[512,512]{1,0:T(8,128)(2,1)S(1)}, bf16[512,512]{1,0:T(8,128)(2,1)S(1)}, f32[1,512]{1,0:T(1,128)S(1)}, bf16[512]{0:T(512)(128)(2,1)S(1)}) custom-call(bf16[512,512]{1,0:T(8,128)(2,1)} %q_hbm.1, bf16[512,512]{1,0:T(8,128)(2,1)} %k_hbm.1, bf16[512,512]{1,0:T(8,128)(2,1)} %v_hbm.1, bf16[512,512]{1,0:T(8,128)(2,1)} %r_hbm.1, ...), custom_call_target="tpu_custom_call" | custom-call | tf_op jit(solution)/shard_map/pallas_call | solution.py:372
  45.6 1.0 %shard_map.105 = (bf16[512,512]{1,0:T(8,128)(2,1)}, bf16[512,512]{1,0:T(8,128)(2,1)}) custom-call(bf16[512,512]{1,0:T(8,128)(2,1)S(1)} %get-tuple-element.6.gated, bf16[512,512]{1,0:T(8,128)(2,1)S(1)} %get-tuple-element.7.resid, f32[1,512]{1,0:T(1,128)S(1)} %get-tuple-element.8.scale_ref, bf16[512]{0:T(512)(128)(2,1)S(1)} %get-tuple-element.9.gain_ref), custom_call_target="tpu_custom_call" | custom-call | tf_op jit(solution)/shard_map/pallas_call | solution.py:410

commit v5 on v4

--- a/solution.py
+++ b/solution.py
@@ -73,6 +73,8 @@
     toep,
     flipped,
     squares,
+    seam,
+    head_only,
     part,
     parts,
     load_sem,
@@ -257,44 +259,62 @@
     in_tile = LANES // GSIZE
     lane_group = lax.broadcasted_iota(jnp.int32, (TAPS, LANES), 1) // GSIZE
 
-    def convolve(pair):
+    def chosen(stack, count):
+        out = stack[0:count]
+        for g in range(1, in_tile):
+            own = lane_group[0:count] == g
+            out = jnp.where(own, stack[g * count : (g + 1) * count], out)
+        return out
+
+    def gate(start, count, lanes, out):
+        rows = pl.ds(start, count)
+        valid = (lax.broadcasted_iota(jnp.int32, (count, LANES), 0) + start) < length
+        mixed = jnp.where(valid, qfeat[rows, lanes] * out, 0.0).astype(BF16)
+        mixed_v[rows, lanes] = mixed
+        total = rbuf[rows, lanes].astype(F32) + mixed.astype(F32)
+        return total * total
+
+    def convolve(blocks, unroll=False):
         def step(b, _):
-            lanes = pl.ds(pl.multiple_of(b * LANES, LANES), LANES)
-            window = jnp.concatenate(
-                [mix[blk * TAPS : (blk + 2) * TAPS, lanes] for blk in pair], axis=1
-            )
-            rows = pl.ds(pl.multiple_of(b * in_tile * TAPS, TAPS), in_tile * TAPS)
-            product_all = jnp.dot(toep[rows, :], window, preferred_element_type=F32)
-            for half, blk in enumerate(pair):
-                side = slice(half * LANES, (half + 1) * LANES)
-                out = product_all[0:TAPS, side]
-                for g in range(1, in_tile):
-                    out = jnp.where(
-                        lane_group == g, product_all[g * TAPS : (g + 1) * TAPS, side], out
-                    )
+            lanes = pl.ds(b * LANES if unroll else pl.multiple_of(b * LANES, LANES), LANES)
+            windows = [mix[blk * TAPS : (blk + 2) * TAPS, lanes] for blk in blocks]
+            first = b * in_tile * TAPS
+            rows = pl.ds(first if unroll else pl.multiple_of(first, TAPS), in_tile * TAPS)
+            window = jnp.concatenate(windows, axis=1)
+            product_all = jnp.concatenate([jnp.dot(
+                toep[pl.ds(first + g * TAPS, TAPS), :], window, preferred_element_type=F32
+            ) for g in range(in_tile)], axis=0)
+            for half, blk in enumerate(blocks):
+                out = chosen(product_all[:, half * LANES : (half + 1) * LANES], TAPS)
+                if blk == 1:
+                    seam[:, lanes] = out[0:16]
                 span = slice(blk * TAPS, (blk + 1) * TAPS)
-                valid = (
-                    lax.broadcasted_iota(jnp.int32, (TAPS, LANES), 0) + blk * TAPS
-                ) < length
-                mixed = jnp.where(valid, qfeat[span, lanes] * out, 0.0).astype(BF16)
-                mixed_v[span, lanes] = mixed
-                total = rbuf[span, lanes].astype(F32) + mixed.astype(F32)
-                squares[span, :] = squares[span, :] + total * total
+                squares[span, :] = squares[span, :] + gate(blk * TAPS, TAPS, lanes, out)
             return 0
 
-        lax.fori_loop(0, tiles, step, 0)
-
+        if unroll:
+            for b in range(tiles):
+                step(b, 0)
+        else:
+            lax.fori_loop(0, tiles, step, 0)
+
+    def row_of_sums(blk):
+        span = slice(blk * TAPS, (blk + 1) * TAPS)
+        part[:, span] = jnp.sum(squares[span, :].T, axis=0, keepdims=True)
+
+    mix[TAPS : TAPS + 16, :] = jnp.zeros((16, WIDTH), BF16)
+    head_only[...] = jnp.zeros((TAPS, WIDTH), BF16)
+    convolve((1,))
     convolve((2, 3))
+    row_of_sums(2)
+    row_of_sums(3)
 
     pltpu.make_async_copy(fin.at[others], fin.at[others], recv2).wait()
 
     keep = (pred_ref[me] >= 0).astype(F32)
 
-    def unpack_fin(p, _):
-        rows_f[pl.ds(pl.multiple_of(4 * p, 4), 4), :] = fin[p, TILE // QUAD].astype(F32) * keep
-        return 0
-
-    lax.fori_loop(0, n_seq, unpack_fin, 0)
+    for p in range(n_seq):
+        rows_f[QUAD * p : QUAD * (p + 1), :] = fin[p, TILE // QUAD].astype(F32) * keep
     for a in range(TAPS // 16):
         for b in range(tiles):
             lanes = slice(b * LANES, (b + 1) * LANES)
@@ -310,14 +330,28 @@
             ).astype(BF16)
     for b in range(tiles):
         lanes = pl.ds(b * LANES, LANES)
-        mix[TAPS : TAPS + 16, lanes] = product(0, 16, lanes)
+        head = product(0, 16, lanes)
+        mix[TAPS : TAPS + 16, lanes] = head
+        head_only[0:16, lanes] = head
         qfeat[0:16, lanes] = featurize(qbuf, 0, 0, 16, lanes)
 
-    convolve((0, 1))
-
-    for blk in range(ROWS // TAPS):
-        span = slice(blk * TAPS, (blk + 1) * TAPS)
-        part[:, span] = jnp.sum(squares[span, :].T, axis=0, keepdims=True)
+    seam_squares = jnp.zeros((16, LANES), F32)
+    for b in range(tiles):
+        lanes = pl.ds(b * LANES, LANES)
+        firsts = [
+            toep[(b * in_tile + g) * TAPS : (b * in_tile + g) * TAPS + 16, 0:TAPS]
+            for g in range(in_tile)
+        ]
+        added = jnp.dot(
+            jnp.concatenate(firsts, axis=0), head_only[:, lanes], preferred_element_type=F32
+        )
+        out = seam[:, lanes] + chosen(added, 16)
+        seam_squares = seam_squares + gate(TAPS, 16, lanes, out)
+    squares[TAPS : TAPS + 16, :] = seam_squares
+
+    convolve((0,), unroll=True)
+    row_of_sums(0)
+    row_of_sums(1)
     parts[mine] = part[...]
 
     for peer in mp_peers:
@@ -388,6 +422,8 @@
             pltpu.VMEM((groups * TAPS, 2 * TAPS), BF16),
             pltpu.VMEM((groups, LANES), F32),
             pltpu.VMEM((ROWS, LANES), F32),
+            pltpu.VMEM((16, WIDTH), F32),
+            pltpu.VMEM((TAPS, WIDTH), BF16),
             pltpu.VMEM((1, ROWS), F32),
             pltpu.VMEM((n_mp, 1, ROWS), F32),
             pltpu.SemaphoreType.DMA((9,)),

time: 46.8 us -> 45.8 us (0.979)
  Pallas kernels: 46 us -> 45 us
    pallas_call x1, Pallas kernels: 45 us -> 44 us  [body(): pl.pallas_call(functools.partial(kernel, n_seq, n_mp), out_shape=(pltpu.V...]
where the time goes in v5:
time: 45.8 us; the launch traced here: 45.7 us
  Pallas kernels  45 us (98%)
  between operations  0.64 us (1%)
    pallas_call x1, Pallas kernels, body(): pl.pallas_call(functools.partial(kernel, n_seq, n_mp), out_shape=(pltpu.V...  44 us
    pallas_call x1, Pallas kernels, body(): pl.pallas_call(finish, out_shape=(out, out), in_specs=[row, row, row, row...  1 us

profile of v5, /device:TPU:1, one launch (start us, length us, event | category | flops | bytes accessed | tf_op | source)
XLA Modules:
  0.0 45.7 jit_solution(13129479150655426960)
XLA Ops:
  0.6 44.0 %shard_map.104 = (bf16[512,512]{1,0:T(8,128)(2,1)S(1)}, bf16[512,512]{1,0:T(8,128)(2,1)S(1)}, f32[1,512]{1,0:T(1,128)S(1)}, bf16[512]{0:T(512)(128)(2,1)S(1)}) custom-call(bf16[512,512]{1,0:T(8,128)(2,1)} %q_hbm.1, bf16[512,512]{1,0:T(8,128)(2,1)} %k_hbm.1, bf16[512,512]{1,0:T(8,128)(2,1)} %v_hbm.1, bf16[512,512]{1,0:T(8,128)(2,1)} %r_hbm.1, ...), custom_call_target="tpu_custom_call" | custom-call | tf_op jit(solution)/shard_map/pallas_call | solution.py:406
  44.7 1.0 %shard_map.105 = (bf16[512,512]{1,0:T(8,128)(2,1)}, bf16[512,512]{1,0:T(8,128)(2,1)}) custom-call(bf16[512,512]{1,0:T(8,128)(2,1)S(1)} %get-tuple-element.6.gated, bf16[512,512]{1,0:T(8,128)(2,1)S(1)} %get-tuple-element.7.resid, f32[1,512]{1,0:T(1,128)S(1)} %get-tuple-element.8.scale_ref, bf16[512]{0:T(512)(128)(2,1)S(1)} %get-tuple-element.9.gain_ref), custom_call_target="tpu_custom_call" | custom-call | tf_op jit(solution)/shard_map/pallas_call | solution.py:446

commit v6 on v5

--- a/solution.py
+++ b/solution.py
@@ -108,8 +108,6 @@
             )
         )
     ]
-    for load in loads:
-        load.start()
     seq_parts, mp_parts = (n_seq // 2, 2), ((n_mp // 4, 2, 2) if n_mp % 4 == 0 else (n_mp,))
     seq_peers = [
         moved(me, seq_parts, offset) for offset in farthest_first(seq_parts, (1, 1))
@@ -119,10 +117,14 @@
         for offset in farthest_first(mp_parts, (2, 4, 1) if n_mp % 4 == 0 else (1,))
     ]
     barrier = pltpu.get_barrier_semaphore()
-    for peer in seq_peers:
+    for peer in seq_peers[:15]:
         pl.semaphore_signal(barrier, inc=1, device_id={"seq": peer}, device_id_type=MESH)
     for peer in mp_peers:
         pl.semaphore_signal(barrier, inc=1, device_id={"mp": peer}, device_id_type=MESH)
+    for peer in seq_peers[15:]:
+        pl.semaphore_signal(barrier, inc=1, device_id={"seq": peer}, device_id_type=MESH)
+    for load in loads:
+        load.start()
 
     def spread_out(source, landing, send_sem, recv_sem, peer):
         pltpu.make_async_remote_copy(

time: 45.8 us -> 45.6 us (level)
  no operation moved by 1% of the time
where the time goes in v6:
time: 45.6 us; the launch traced here: 45.5 us
  Pallas kernels  44.8 us (98%)
  between operations  0.64 us (1%)
    pallas_call x1, Pallas kernels, body(): pl.pallas_call(functools.partial(kernel, n_seq, n_mp), out_shape=(pltpu.V...  43.8 us
    pallas_call x1, Pallas kernels, body(): pl.pallas_call(finish, out_shape=(out, out), in_specs=[row, row, row, row...  1 us

profile of v6, /device:TPU:1, one launch (start us, length us, event | category | flops | bytes accessed | tf_op | source)
XLA Modules:
  0.0 45.5 jit_solution(18317656822458294851)
XLA Ops:
  0.6 43.8 %shard_map.104 = (bf16[512,512]{1,0:T(8,128)(2,1)S(1)}, bf16[512,512]{1,0:T(8,128)(2,1)S(1)}, f32[1,512]{1,0:T(1,128)S(1)}, bf16[512]{0:T(512)(128)(2,1)S(1)}) custom-call(bf16[512,512]{1,0:T(8,128)(2,1)} %q_hbm.1, bf16[512,512]{1,0:T(8,128)(2,1)} %k_hbm.1, bf16[512,512]{1,0:T(8,128)(2,1)} %v_hbm.1, bf16[512,512]{1,0:T(8,128)(2,1)} %r_hbm.1, ...), custom_call_target="tpu_custom_call" | custom-call | tf_op jit(solution)/shard_map/pallas_call | solution.py:408
  44.5 1.0 %shard_map.105 = (bf16[512,512]{1,0:T(8,128)(2,1)}, bf16[512,512]{1,0:T(8,128)(2,1)}) custom-call(bf16[512,512]{1,0:T(8,128)(2,1)S(1)} %get-tuple-element.6.gated, bf16[512,512]{1,0:T(8,128)(2,1)S(1)} %get-tuple-element.7.resid, f32[1,512]{1,0:T(1,128)S(1)} %get-tuple-element.8.scale_ref, bf16[512]{0:T(512)(128)(2,1)S(1)} %get-tuple-element.9.gain_ref), custom_call_target="tpu_custom_call" | custom-call | tf_op jit(solution)/shard_map/pallas_call | solution.py:448

commit v7 on v6

--- a/solution.py
+++ b/solution.py
@@ -337,6 +337,9 @@
         head_only[0:16, lanes] = head
         qfeat[0:16, lanes] = featurize(qbuf, 0, 0, 16, lanes)
 
+    convolve((0,), unroll=True)
+    row_of_sums(0)
+
     seam_squares = jnp.zeros((16, LANES), F32)
     for b in range(tiles):
         lanes = pl.ds(b * LANES, LANES)
@@ -351,8 +354,6 @@
         seam_squares = seam_squares + gate(TAPS, 16, lanes, out)
     squares[TAPS : TAPS + 16, :] = seam_squares
 
-    convolve((0,), unroll=True)
-    row_of_sums(0)
     row_of_sums(1)
     parts[mine] = part[...]
 

time: 45.6 us -> 45.6 us (level)
  no operation moved by 1% of the time
where the time goes in v7:
time: 45.6 us; the launch traced here: 45.5 us
  Pallas kernels  44.8 us (98%)
  between operations  0.64 us (1%)
    pallas_call x1, Pallas kernels, body(): pl.pallas_call(functools.partial(kernel, n_seq, n_mp), out_shape=(pltpu.V...  43.8 us
    pallas_call x1, Pallas kernels, body(): pl.pallas_call(finish, out_shape=(out, out), in_specs=[row, row, row, row...  1 us

profile of v7, /device:TPU:1, one launch (start us, length us, event | category | flops | bytes accessed | tf_op | source)
XLA Modules:
  0.0 45.5 jit_solution(4925494111419705624)
XLA Ops:
  0.6 43.8 %shard_map.104 = (bf16[512,512]{1,0:T(8,128)(2,1)S(1)}, bf16[512,512]{1,0:T(8,128)(2,1)S(1)}, f32[1,512]{1,0:T(1,128)S(1)}, bf16[512]{0:T(512)(128)(2,1)S(1)}) custom-call(bf16[512,512]{1,0:T(8,128)(2,1)} %q_hbm.1, bf16[512,512]{1,0:T(8,128)(2,1)} %k_hbm.1, bf16[512,512]{1,0:T(8,128)(2,1)} %v_hbm.1, bf16[512,512]{1,0:T(8,128)(2,1)} %r_hbm.1, ...), custom_call_target="tpu_custom_call" | custom-call | tf_op jit(solution)/shard_map/pallas_call | solution.py:409
  44.5 1.0 %shard_map.105 = (bf16[512,512]{1,0:T(8,128)(2,1)}, bf16[512,512]{1,0:T(8,128)(2,1)}) custom-call(bf16[512,512]{1,0:T(8,128)(2,1)S(1)} %get-tuple-element.6.gated, bf16[512,512]{1,0:T(8,128)(2,1)S(1)} %get-tuple-element.7.resid, f32[1,512]{1,0:T(1,128)S(1)} %get-tuple-element.8.scale_ref, bf16[512]{0:T(512)(128)(2,1)S(1)} %get-tuple-element.9.gain_ref), custom_call_target="tpu_custom_call" | custom-call | tf_op jit(solution)/shard_map/pallas_call | solution.py:449
